TPU v7x, 512 devices: a whole 4x4x16 slice. The times are simulated.
512 devices in a mesh: op: 64 (over z, y), sec: 8 (over x, core).
Axes of the slice: x: 4, y: 4, z: 16, core: 2. Of those that a mesh axis runs over, the one named last changes fastest.
Arguments:
- psi: bfloat16 [8, 384, 384], P('sec'), may hold values from -6 to 6
- left_ops: bfloat16 [3584, 384, 384], P(('op', 'sec')), may hold values from -0.3125 to 0.3125
- right_ops: bfloat16 [3584, 384, 384], P(('op', 'sec')), may hold values from -0.0234375 to 0.0234375
- term_src: int32 [3584], P(('op', 'sec')), may hold values from 0 to 7, as said below
- term_count: int32 [64, 8], P('op', 'sec'), may hold values from 1 to 7, as said below
Outputs:
- sigma: bfloat16 [8, 384, 384], P('sec')
Inputs may be any that keep to these rules, and one draw needn't show every extreme that they name: `term_src`: the source sector of a slot of target sector g is g - 1, g or g + 1. `term_count`: at least one device has all 7 slots live in every draw.
All inputs are finite; a program needn't handle non-finite values.
Results may differ from a plain program's by a relative error of at most 0.0051.
Values may be sent and summed in bfloat16 or wider, within the bound.
A program may use at most 64 MiB of HBM per device.

v0:
```python
import jax
import jax.numpy as jnp
from jax import lax
from jax.sharding import PartitionSpec as P


def padded(x, sides, width):
    for axis, dim in sides:
        count, length = (lax.axis_size(axis), x.shape[dim])
        up = [(i, (i + 1) % count) for i in range(count - 1)]
        down = [(j, i) for i, j in up]
        last = lax.slice_in_dim(x, length - width, length, axis=dim)
        first = lax.slice_in_dim(x, 0, width, axis=dim)
        before = lax.ppermute(last, axis, up)
        after = lax.ppermute(first, axis, down)
        x = jnp.concatenate([before, x, after], axis=dim)
    return x


def local(psi, left_ops, right_ops, term_src, term_count):
    blocks = psi.shape[1]
    nearby = padded(psi, (("sec", 0),), 1)
    position = lax.axis_index("sec")
    local_src = term_src - position + 1
    count = term_count[0, 0]

    def term_value(slot):
        block = lax.dynamic_index_in_dim(nearby, local_src[slot], 0, keepdims=False)
        right = lax.dynamic_index_in_dim(right_ops, slot, 0, keepdims=False)
        left = lax.dynamic_index_in_dim(left_ops, slot, 0, keepdims=False)
        inner = jnp.dot(block, right, preferred_element_type=jnp.float32).astype(jnp.bfloat16)
        return jnp.dot(left, inner, preferred_element_type=jnp.float32)

    start = jnp.zeros((blocks, blocks), jnp.float32)
    partial_sum = lax.fori_loop(0, count, lambda slot, acc: acc + term_value(slot), start)
    summed = lax.psum(partial_sum, "op")
    return summed.astype(jnp.bfloat16).reshape(1, blocks, blocks)


def solution(mesh):
    in_specs = (
        P("sec", None, None),
        P(("op", "sec"), None, None),
        P(("op", "sec"), None, None),
        P(("op", "sec")),
        P("op", "sec"),
    )
    out_specs = P("sec", None, None)
    return jax.shard_map(local, mesh=mesh, in_specs=in_specs, out_specs=out_specs, check_vma=False)
```

profile of v0, /device:TPU:6, one launch (start us, length us, event | category | flops | bytes accessed | tf_op | source)
XLA Modules:
  0.0 318.3 jit_solution(15461533104860991567)
XLA Ops:
  0.0 1.9 collective-permute-start
  1.9 3.6 %collective-permute-start.1 = (bf16[1,384,384]{2,1,0:T(8,128)(2,1)}, bf16[1,384,384]{2,1,0:T(8,128)(2,1)S(1)}, u32[]{:S(2)}, u32[]{:S(2)}) collective-permute-start(bf16[1,384,384]{2,1,0:T(8,128)(2,1)} %param.7), channel_id=1, source_target_pairs={{1,0},{2,1},{3,2},{4,3},{5,4},{6,5},{7,6},{9,8},{10,9},{11,10},{12... | collective-permute-start | bytes 884744 | tf_op jit(solution)/shard_map/ppermute | solution.py:15
  5.6 0.7 subtract_add_fusion
  6.2 2.0 collective-permute-done
  8.2 1.9 collective-permute-done.1
  10.1 1.1 pad_maximum_fusion
  11.2 10.0 %while.10 = (s32[]{:T(128)}, f32[384,384]{1,0:T(8,128)S(1)}, s32[]{:T(128)}, bf16[7,384,384]{2,1,0:T(8,128)(2,1)}, s32[7]{0:T(128)S(1)}, /*index=5*/bf16[3,384,3...) while((s32[]{:T(128)}, f32[384,384]{1,0:T(8,128)S(1)}, ...), condition=%wide.region_1.2_spmd, body=%wide.region_0.1_spmd.sunk | while | flops 226787328 | bytes 2066117 | solution.py:35
  11.9 0.6 dynamic_slice.35
  14.2 1.7 convolution_add_fusion.2
  16.6 0.6 dynamic_slice.35
  18.8 1.7 convolution_add_fusion.2
  21.2 297.1 %all-reduce.1 = bf16[384,384]{1,0:T(8,128)(2,1)} all-reduce(f32[384,384]{1,0:T(8,128)S(1)} %get-tuple-element.43), channel_id=1, replica_groups=mesh['op'=64,'sec'=8] {'op'}, use_global_device_ids=true, to_apply=%region_2.3 | all-reduce | flops 147456 | bytes 884736 | tf_op jit(solution)/shard_map/psum | solution.py:36
  (1 shorter events, 0.0 us)
Async XLA Ops:
  0.0 8.2 %collective-permute-start = (bf16[1,384,384]{2,1,0:T(8,128)(2,1)}, bf16[1,384,384]{2,1,0:T(8,128)(2,1)S(1)}, u32[]{:S(2)}, u32[]{:S(2)}) collective-permute-start(bf16[1,384,384]{2,1,0:T(8,128)(2,1)} %param.7), channel_id=1, source_target_pairs={{0,1},{1,2},{2,3},{3,4},{4,5},{5,6},{6,7},{8,9},{9,10},{10,11},{11... | collective-permute-start | bytes 884744 | tf_op jit(solution)/shard_map/ppermute | solution.py:14
  1.9 8.2 %collective-permute-start.1 = (bf16[1,384,384]{2,1,0:T(8,128)(2,1)}, bf16[1,384,384]{2,1,0:T(8,128)(2,1)S(1)}, u32[]{:S(2)}, u32[]{:S(2)}) collective-permute-start(bf16[1,384,384]{2,1,0:T(8,128)(2,1)} %param.7), channel_id=1, source_target_pairs={{1,0},{2,1},{3,2},{4,3},{5,4},{6,5},{7,6},{9,8},{10,9},{11,10},{12... | collective-permute-start | bytes 884744 | tf_op jit(solution)/shard_map/ppermute | solution.py:15
where the time goes:
time: 319 us; the launch traced here: 318 us
  blocking collectives  297 us (93%)
  starting transfers between devices  5.55 us (2%)
  loops' own time  5.36 us (2%)
  waiting for transfers between devices  3.87 us (1%)
  matrix products  3.46 us (1%)
    psum x1, blocking collectives, local(): summed = lax.psum(partial_sum, 'op')  297 us
  transfers between devices with their start and end apart: 2, of which 2 were waited for; matrix products, arithmetic and copies ran while one was open for 0% of the time, Pallas kernels for 0%

commit v1 on v0

v1 whole, which is shorter than its diff:
```python
import jax
import jax.numpy as jnp
from jax import lax
from jax.experimental import pallas as pl
from jax.experimental.pallas import tpu as pltpu
from jax.sharding import PartitionSpec as P

MESH = pl.DeviceIdType.MESH
NY, NZ, NSEC = 4, 16, 8
M, SLOTS = 384, 7
OWNERS, ROWS = 12, 8
FAR_FIRST = (8, 7, 9, 6, 10, 5, 11, 4, 12, 3, 13, 2, 14, 1, 15)
Y_FIRST = (2, 1, 3)


def kernel(
    psi, left, right, src, count, out,
    near, lbuf, rbuf, acc, pbuf, yrecv, zbuf, zrecv, quarter,
    psi_sem, l_sem, r_sem, psi_send, psi_recv,
    ys_sem, yr_sem, zs_sem, zr_sem, gs_sem, gr_sem, hs_sem, hr_sem, out_sem,
):
    op, sec = lax.axis_index("op"), lax.axis_index("sec")
    z, y = op // NY, op % NY

    def at_y(d):
        return (z * NY + (y + d) % NY, sec)

    def at_z(d):
        return ((z + d) % NZ * NY + y, sec)

    def at_sec(d):
        return (op, (sec + d) % NSEC)

    def remote(a, b, s, r, device):
        return pltpu.make_async_remote_copy(
            src_ref=a, dst_ref=b, send_sem=s, recv_sem=r,
            device_id=device, device_id_type=MESH,
        )

    own = pltpu.make_async_copy(psi.at[0], near.at[1], psi_sem)
    own.start()
    loads_r = [pltpu.make_async_copy(right.at[t], rbuf.at[t], r_sem.at[t]) for t in range(SLOTS)]
    loads_l = [pltpu.make_async_copy(left.at[t], lbuf.at[t], l_sem.at[t]) for t in range(SLOTS)]
    for t in range(SLOTS):
        loads_r[t].start()
        loads_l[t].start()

    peers = [at_sec(1), at_sec(-1)] + [at_y(d) for d in Y_FIRST] + [at_z(d) for d in FAR_FIRST]
    barrier = pltpu.get_barrier_semaphore()
    for peer in reversed(peers):
        pl.semaphore_signal(barrier, inc=1, device_id=peer, device_id_type=MESH)
    pl.semaphore_wait(barrier, len(peers))

    up = remote(psi.at[0], near.at[0], psi_send.at[0], psi_recv.at[0], at_sec(1))
    down = remote(psi.at[0], near.at[2], psi_send.at[1], psi_recv.at[1], at_sec(-1))
    up.start()
    down.start()
    own.wait()
    up.wait_recv()
    down.wait_recv()

    live = count[0, 0]
    for t in range(SLOTS):
        loads_r[t].wait()
        block = near[jnp.clip(src[t] - sec + 1, 0, 2)]
        inner = jnp.dot(block, rbuf[t], preferred_element_type=jnp.float32)
        inner = jnp.where(t < live, inner, 0.0).astype(jnp.bfloat16)
        loads_l[t].wait()
        term = jnp.dot(lbuf[t], inner, preferred_element_type=jnp.float32)
        term = term.reshape(NY, OWNERS, ROWS, M)
        if t == 0:
            acc[...] = term
        elif t < SLOTS - 1:
            acc[...] += term
        else:
            total = acc[...] + term
            acc[...] = total
            pbuf[...] = total.astype(jnp.bfloat16)

    copies = []
    for d in Y_FIRST:
        c = remote(pbuf.at[(y + d) % NY], yrecv.at[d - 1], ys_sem.at[d - 1], yr_sem.at[d - 1], at_y(d))
        c.start()
        copies.append(c)
    for c in copies:
        c.wait_recv()
    summed = acc[y]
    for d in range(1, NY):
        summed = summed + yrecv[d - 1].astype(jnp.float32)
    zbuf[...] = summed.astype(jnp.bfloat16)

    def piece(d):
        p = (z + d) % NZ
        return p < OWNERS, remote(zbuf.at[p % OWNERS], zrecv.at[d - 1], zs_sem.at[d - 1], zr_sem.at[d - 1], at_z(d))

    for d in FAR_FIRST:
        ok, c = piece(d)

        @pl.when(ok)
        def _():
            c.start()

    def spread(d):
        return remote(quarter.at[z % OWNERS], quarter.at[z % OWNERS], gs_sem.at[d - 1], gr_sem.at[z % OWNERS], at_z(d))

    @pl.when(z < OWNERS)
    def _():
        total = zbuf[z % OWNERS].astype(jnp.float32)
        for d in reversed(FAR_FIRST):
            piece(d)[1].wait_recv()
            total = total + zrecv[d - 1].astype(jnp.float32)
        quarter[z % OWNERS] = total.astype(jnp.bfloat16)
        for d in FAR_FIRST:
            spread(d).start()

    for p in range(OWNERS):
        @pl.when(p != z)
        def _():
            remote(quarter.at[p], quarter.at[p], gs_sem.at[0], gr_sem.at[p], at_z(1)).wait_recv()

    for d in Y_FIRST:
        c = remote(quarter, out.at[y], hs_sem.at[d - 1], hr_sem.at[d - 1], at_y(d))
        c.start()
        copies.append(c)
    mine = pltpu.make_async_copy(quarter, out.at[y], out_sem)
    mine.start()

    up.wait_send()
    down.wait_send()
    for c in copies[:3]:
        c.wait_send()
    for d in FAR_FIRST:
        ok, c = piece(d)

        @pl.when(ok)
        def _():
            c.wait_send()

    @pl.when(z < OWNERS)
    def _():
        for d in FAR_FIRST:
            spread(d).wait_send()

    mine.wait()
    for c in copies[3:]:
        c.wait()


def local(psi, left_ops, right_ops, term_src, term_count):
    hbm = pl.BlockSpec(memory_space=pl.ANY)
    smem = pl.BlockSpec(memory_space=pltpu.SMEM)
    dma = pltpu.SemaphoreType.DMA
    bf16, f32 = jnp.bfloat16, jnp.float32
    out = pl.pallas_call(
        kernel,
        out_shape=jax.ShapeDtypeStruct((NY, OWNERS, ROWS, M), bf16),
        in_specs=[hbm, hbm, hbm, smem, smem],
        out_specs=hbm,
        scratch_shapes=[
            pltpu.VMEM((3, M, M), bf16),
            pltpu.VMEM((SLOTS, M, M), bf16),
            pltpu.VMEM((SLOTS, M, M), bf16),
            pltpu.VMEM((NY, OWNERS, ROWS, M), f32),
            pltpu.VMEM((NY, OWNERS, ROWS, M), bf16),
            pltpu.VMEM((NY - 1, OWNERS, ROWS, M), bf16),
            pltpu.VMEM((OWNERS, ROWS, M), bf16),
            pltpu.VMEM((NZ - 1, ROWS, M), bf16),
            pltpu.VMEM((OWNERS, ROWS, M), bf16),
            dma, dma((SLOTS,)), dma((SLOTS,)), dma((2,)), dma((2,)),
            dma((NY - 1,)), dma((NY - 1,)),
            dma((NZ - 1,)), dma((NZ - 1,)),
            dma((NZ - 1,)), dma((OWNERS,)),
            dma((NY - 1,)), dma((NY - 1,)), dma,
        ],
        compiler_params=pltpu.CompilerParams(
            collective_id=0, has_side_effects=True, vmem_limit_bytes=60 * 1024 * 1024
        ),
        cost_estimate=pl.CostEstimate(
            flops=4 * SLOTS * M**3, bytes_accessed=4 * SLOTS * M * M, transcendentals=0
        ),
        name="sigma_sum",
    )(psi, left_ops, right_ops, term_src, term_count)
    return out.reshape(1, M, M)


def solution(mesh):
    in_specs = (
        P("sec", None, None),
        P(("op", "sec"), None, None),
        P(("op", "sec"), None, None),
        P(("op", "sec")),
        P("op", "sec"),
    )
    out_specs = P("sec", None, None)
    return jax.shard_map(local, mesh=mesh, in_specs=in_specs, out_specs=out_specs, check_vma=False)
```

time: 319 us -> 55.1 us (0.17)
  the two profiles are of different devices: /device:TPU:6 before, /device:TPU:8 now
where the time goes in v1:
time: 55.1 us; the launch traced here: 55 us
  Pallas kernels  52.6 us (95%)
  local copies, waits for them, and re-layouts  1.71 us (3%)
  between operations  0.66 us (1%)
    pallas_call x1, Pallas kernels, local(): pl.pallas_call(kernel, out_shape=jax.ShapeDtypeStruct((NY, OWNERS, ROWS,...  52.6 us
    unnamed x1, local copies, waits for them, and re-layouts  1.71 us

profile of v1, /device:TPU:8, one launch (start us, length us, event | category | flops | bytes accessed | tf_op | source)
XLA Modules:
  0.0 55.0 jit_solution(4446493309706446178)
XLA Ops:
  0.7 52.6 %sigma_sum.1 = bf16[4,12,8,384]{3,2,1,0:T(8,128)(2,1)} custom-call(bf16[1,384,384]{2,1,0:T(8,128)(2,1)} %psi.1, bf16[7,384,384]{2,1,0:T(8,128)(2,1)} %left.1, bf16[7,384,384]{2,1,0:T(8,128)(2,1)} %right.1, s32[7]{0:T(128)} %src.1, s32[1,1]{1,0:T(1,128)S(6)} %copy.7.count), custom_call_target="tpu_custom_call" | custom-call | flops 1585446912 | bytes 4128768 | tf_op jit(solution)/shard_map/sigma_sum/pallas_call | solution.py:154
  53.2 1.7 %copy.8 = bf16[1,384,384]{2,1,0:T(8,128)(2,1)} copy(bf16[1,384,384]{2,1,0:T(8,128)(2,1)} %bitcast.1) | data formatting | bytes 589824

commit v2 on v1

v2 whole, which is shorter than its diff:
```python
import jax
import jax.numpy as jnp
from jax import lax
from jax.experimental import pallas as pl
from jax.experimental.pallas import tpu as pltpu
from jax.sharding import PartitionSpec as P

MESH = pl.DeviceIdType.MESH
NY, NZ, NSEC = 4, 16, 8
M, SLOTS = 384, 7
NB, OWN, ROWS = 4, 3, 8
FAR_FIRST = (8, 7, 9, 6, 10, 5, 11, 4, 12, 3, 13, 2, 14, 1, 15)
FAR_BLOCKS = (2, 1, 3, 0)
Y_FIRST = (2, 1, 3)


def kernel(
    psi, left, right, src, count, out,
    near, lbuf, rbuf, icat, pbuf, yrecv, zbuf, zrecv, quarter,
    psi_sem, l_sem, r_sem, psi_send, psi_recv,
    ys_sem, yr_sem, zs_sem, zr_sem, gs_sem, gr_sem, hs_sem, hr_sem, out_sem,
    know_a, know_b, know_c,
):
    op, sec = lax.axis_index("op"), lax.axis_index("sec")
    z, y = op // NY, op % NY
    zb, zk = z // NB, z % NB

    def at_y(d):
        return (z * NY + (y + d) % NY, sec)

    def at_z(d):
        return ((z + d) % NZ * NY + y, sec)

    def at_sec(d):
        return (op, (sec + d) % NSEC)

    def remote(a, b, s, r, device):
        return pltpu.make_async_remote_copy(
            src_ref=a, dst_ref=b, send_sem=s, recv_sem=r,
            device_id=device, device_id_type=MESH,
        )

    def signal(sem, device):
        pl.semaphore_signal(sem, inc=1, device_id=device, device_id_type=MESH)

    barrier = pltpu.get_barrier_semaphore()
    beside = [at_z(1), at_z(-1), at_y(1), at_y(-1)]
    for peer in [at_sec(1), at_sec(-1)] + beside:
        signal(barrier, peer)

    own = pltpu.make_async_copy(psi.at[0], near.at[1], psi_sem)
    own.start()
    loads = []
    for t in range(SLOTS):
        loads.append(pltpu.make_async_copy(right.at[t], rbuf.at[t], r_sem.at[t]))
    for t in range(SLOTS):
        loads.append(pltpu.make_async_copy(left.at[t], lbuf.at[:, pl.ds(t * M, M)], l_sem.at[t]))
    for c in loads:
        c.start()

    pl.semaphore_wait(barrier, 6)
    up = remote(psi.at[0], near.at[0], psi_send.at[0], psi_recv.at[0], at_sec(1))
    down = remote(psi.at[0], near.at[2], psi_send.at[1], psi_recv.at[1], at_sec(-1))
    up.start()
    down.start()
    for peer in beside:
        signal(know_a, peer)
    own.wait()
    for c in loads:
        c.wait()
    pl.semaphore_wait(know_a, 4)
    for d in (2, -2):
        signal(know_b, at_z(d))
    up.wait_recv()
    down.wait_recv()

    live = count[0, 0]
    for t in range(SLOTS):
        block = near[jnp.clip(src[t] - sec + 1, 0, 2)]
        inner = jnp.dot(block, rbuf[t], preferred_element_type=jnp.float32)
        icat[pl.ds(t * M, M)] = jnp.where(t < live, inner, 0.0).astype(jnp.bfloat16)
    total = jnp.dot(lbuf[...], icat[...], preferred_element_type=jnp.float32)
    pbuf[...] = total.astype(jnp.bfloat16).reshape(NY, NB, OWN, ROWS, M)

    y_copies = []
    for e in FAR_BLOCKS:
        b = (zb + e) % NB
        row = []
        for d in Y_FIRST:
            c = remote(
                pbuf.at[(y + d) % NY, b], yrecv.at[d - 1, b],
                ys_sem.at[d - 1, e], yr_sem.at[d - 1, e], at_y(d),
            )
            c.start()
            row.append(c)
        y_copies.append(row)
    pl.semaphore_wait(know_b, 2)
    for d in (4, -4):
        signal(know_c, at_z(d))

    def piece(e, k):
        b = (zb + e) % NB
        owner = b * NB + k
        return remote(
            zbuf.at[b, k], zrecv.at[z], zs_sem.at[e, k], zr_sem.at[z], (owner * NY + y, sec)
        )

    for i, e in enumerate(FAR_BLOCKS):
        b = (zb + e) % NB
        for c in y_copies[i]:
            c.wait_recv()
        total = pbuf[y, b].astype(jnp.float32)
        for d in range(1, NY):
            total = total + yrecv[d - 1, b].astype(jnp.float32)
        zbuf[b] = total.astype(jnp.bfloat16)
        if i == 0:
            pl.semaphore_wait(know_c, 2)
        for k in range(OWN):
            if e == 0:
                @pl.when(k != zk)
                def _():
                    piece(e, k).start()
            else:
                piece(e, k).start()

    def spread(d):
        mine = quarter.at[zb, zk % OWN]
        return remote(mine, mine, gs_sem.at[d - 1], gr_sem.at[zb, zk % OWN], at_z(d))

    @pl.when(zk < OWN)
    def _():
        total = zbuf[zb, zk % OWN].astype(jnp.float32)
        for d in reversed(FAR_FIRST):
            s = (z + d) % NZ
            remote(zbuf.at[0, 0], zrecv.at[s], zs_sem.at[0, 0], zr_sem.at[s], at_z(1)).wait_recv()
            total = total + zrecv[s].astype(jnp.float32)
        quarter[zb, zk % OWN] = total.astype(jnp.bfloat16)
        for d in FAR_FIRST:
            spread(d).start()

    h_copies = []
    for e in reversed(FAR_BLOCKS):
        b = (zb + e) % NB
        for k in range(OWN):
            def arrived():
                part = quarter.at[b, k]
                remote(part, part, gs_sem.at[0], gr_sem.at[b, k], at_z(1)).wait_recv()

            if e == 0:
                pl.when(k != zk)(arrived)
            else:
                arrived()
        for d in Y_FIRST:
            c = remote(
                quarter.at[b], out.at[y, b], hs_sem.at[d - 1, e], hr_sem.at[d - 1, e], at_y(d)
            )
            c.start()
            h_copies.append(c)
        c = pltpu.make_async_copy(quarter.at[b], out.at[y, b], out_sem.at[e])
        c.start()
        h_copies.append(c)

    up.wait_send()
    down.wait_send()
    for row in y_copies:
        for c in row:
            c.wait_send()
    for e in FAR_BLOCKS:
        for k in range(OWN):
            if e == 0:
                @pl.when(k != zk)
                def _():
                    piece(e, k).wait_send()
            else:
                piece(e, k).wait_send()

    @pl.when(zk < OWN)
    def _():
        for d in FAR_FIRST:
            spread(d).wait_send()

    for c in h_copies:
        c.wait()


def local(psi, left_ops, right_ops, term_src, term_count):
    hbm = pl.BlockSpec(memory_space=pl.ANY)
    smem = pl.BlockSpec(memory_space=pltpu.SMEM)
    dma, plain = pltpu.SemaphoreType.DMA, pltpu.SemaphoreType.REGULAR
    bf16 = jnp.bfloat16
    out = pl.pallas_call(
        kernel,
        out_shape=jax.ShapeDtypeStruct((NY, NB, OWN, ROWS, M), bf16),
        in_specs=[hbm, hbm, hbm, smem, smem],
        out_specs=hbm,
        scratch_shapes=[
            pltpu.VMEM((3, M, M), bf16),
            pltpu.VMEM((M, SLOTS * M), bf16),
            pltpu.VMEM((SLOTS, M, M), bf16),
            pltpu.VMEM((SLOTS * M, M), bf16),
            pltpu.VMEM((NY, NB, OWN, ROWS, M), bf16),
            pltpu.VMEM((NY - 1, NB, OWN, ROWS, M), bf16),
            pltpu.VMEM((NB, OWN, ROWS, M), bf16),
            pltpu.VMEM((NZ, ROWS, M), bf16),
            pltpu.VMEM((NB, OWN, ROWS, M), bf16),
            dma, dma((SLOTS,)), dma((SLOTS,)), dma((2,)), dma((2,)),
            dma((NY - 1, NB)), dma((NY - 1, NB)),
            dma((NB, OWN)), dma((NZ,)),
            dma((NZ - 1,)), dma((NB, OWN)),
            dma((NY - 1, NB)), dma((NY - 1, NB)), dma((NB,)),
            plain, plain, plain,
        ],
        compiler_params=pltpu.CompilerParams(
            collective_id=0, has_side_effects=True, vmem_limit_bytes=60 * 1024 * 1024
        ),
        cost_estimate=pl.CostEstimate(
            flops=4 * SLOTS * M**3, bytes_accessed=4 * SLOTS * M * M, transcendentals=0
        ),
        name="sigma_sum",
    )(psi, left_ops, right_ops, term_src, term_count)
    return out.reshape(1, M, M)


def solution(mesh):
    in_specs = (
        P("sec", None, None),
        P(("op", "sec"), None, None),
        P(("op", "sec"), None, None),
        P(("op", "sec")),
        P("op", "sec"),
    )
    out_specs = P("sec", None, None)
    return jax.shard_map(local, mesh=mesh, in_specs=in_specs, out_specs=out_specs, check_vma=False)
```

time: 55.1 us -> 46.7 us (0.85)
  the two profiles are of different devices: /device:TPU:8 before, /device:TPU:6 now
where the time goes in v2:
time: 46.7 us; the launch traced here: 46.6 us
  Pallas kernels  44.2 us (95%)
  local copies, waits for them, and re-layouts  1.71 us (4%)
  between operations  0.66 us (1%)
    pallas_call x1, Pallas kernels, local(): pl.pallas_call(kernel, out_shape=jax.ShapeDtypeStruct((NY, NB, OWN, ROWS,...  44.2 us
    unnamed x1, local copies, waits for them, and re-layouts  1.71 us

profile of v2, /device:TPU:6, one launch (start us, length us, event | category | flops | bytes accessed | tf_op | source)
XLA Modules:
  0.0 46.6 jit_solution(300929458189378641)
XLA Ops:
  0.7 44.2 %sigma_sum.1 = bf16[4,4,3,8,384]{4,3,2,1,0:T(8,128)(2,1)} custom-call(bf16[1,384,384]{2,1,0:T(8,128)(2,1)} %psi.1, bf16[7,384,384]{2,1,0:T(8,128)(2,1)} %left.1, bf16[7,384,384]{2,1,0:T(8,128)(2,1)} %right.1, s32[7]{0:T(128)} %src.1, s32[1,1]{1,0:T(1,128)S(6)} %copy.7.count), custom_call_target="tpu_custom_call" | custom-call | flops 1585446912 | bytes 4128768 | tf_op jit(solution)/shard_map/sigma_sum/pallas_call | solution.py:191
  44.9 1.7 %copy.8 = bf16[1,384,384]{2,1,0:T(8,128)(2,1)} copy(bf16[1,384,384]{2,1,0:T(8,128)(2,1)} %bitcast.1) | data formatting | bytes 589824

commit v3 on v2

v3 whole, which is shorter than its diff:
```python
import jax
import jax.numpy as jnp
from jax import lax
from jax.experimental import pallas as pl
from jax.experimental.pallas import tpu as pltpu
from jax.sharding import PartitionSpec as P

MESH = pl.DeviceIdType.MESH
NY, NZ, NSEC = 4, 16, 8
M, SLOTS = 384, 7
PARTS = ((0, 256), (256, 128))
NB, OWN, ROWS, FIRST = 4, 3, 8, 10
NEAR_FIRST = (1, 15, 2, 14, 3, 13, 4, 12, 5, 11, 6, 10, 7, 9, 8)
FAR_BLOCKS = (
    (3, 2, 1, 0), (3, 2, 0, 1), (0, 3, 1, 2), (0, 1, 2, 3), (1, 0, 2, 3), (1, 2, 0, 3), (2, 1, 3, 0), (2, 3, 1, 0),
)
SPREAD = (0, 1, 2, 3, 4, 5, 6, 7, 15, 14, 13, 12, 8, 11, 9, 10)
Y_FIRST = (2, 1, 3)


def kernel(
    psi, left, right, src_in, count_in, out, src, count,
    near_a, near_b, lbuf, rbuf, icat, acc, pbuf, yrecv, zbuf, zrecv, quarter,
    psi_sem, l_sem, r_sem, psi_send, psi_recv,
    ys_sem, yr_sem, zs_sem, zr_sem, gs_sem, gr_sem, hs_sem, hr_sem, out_sem,
    know_a, know_b, know_c, scalar_sem,
):
    op, sec = lax.axis_index("op"), lax.axis_index("sec")
    z, y = op // NY, op % NY
    mine = (z + NZ - FIRST) % NZ
    is_owner = mine < NB * OWN
    mb, mk = mine // OWN % NB, mine % OWN
    group = jnp.where(is_owner, mine // OWN, mine - NB * OWN + NB)
    blocks = []
    for i in range(NB):
        block = FAR_BLOCKS[0][i]
        for g in range(1, 2 * NB):
            block = jnp.where(group == g, FAR_BLOCKS[g][i], block)
        blocks.append(block)

    def at_y(d):
        return (z * NY + (y + d) % NY, sec)

    def at_z(d):
        return ((z + d) % NZ * NY + y, sec)

    def at_sec(d):
        return (op, (sec + d) % NSEC)

    def remote(a, b, s, r, device):
        return pltpu.make_async_remote_copy(
            src_ref=a, dst_ref=b, send_sem=s, recv_sem=r,
            device_id=device, device_id_type=MESH,
        )

    def signal(sem, device):
        pl.semaphore_signal(sem, inc=1, device_id=device, device_id_type=MESH)

    barrier = pltpu.get_barrier_semaphore()
    beside = [at_z(1), at_z(-1), at_y(1), at_y(-1)]
    for peer in beside:
        signal(barrier, peer)
    has_up, has_down = sec < NSEC - 1, sec > 0

    @pl.when(has_up)
    def _():
        signal(barrier, at_sec(1))

    @pl.when(has_down)
    def _():
        signal(barrier, at_sec(-1))

    near = (near_a, near_b)
    own = [
        pltpu.make_async_copy(psi.at[0, pl.ds(*part)], near[p].at[1], psi_sem.at[p])
        for p, part in enumerate(PARTS)
    ]
    for c in own:
        c.start()
    loads = [
        pltpu.make_async_copy(src_in, src, scalar_sem.at[0]),
        pltpu.make_async_copy(count_in, count, scalar_sem.at[1]),
    ]
    for t in range(SLOTS):
        loads.append(pltpu.make_async_copy(right.at[t], rbuf.at[t], r_sem.at[t]))
    for p, (first, rows) in enumerate(PARTS):
        for t in range(SLOTS):
            loads.append(pltpu.make_async_copy(
                left.at[t, :, pl.ds(first, rows)],
                lbuf.at[:, pl.ds(SLOTS * first + t * rows, rows)],
                l_sem.at[p, t],
            ))

    ends = ((sec == 0) | (sec == NSEC - 1)).astype(jnp.int32)
    pl.semaphore_wait(barrier, 6 - ends)
    for c in own:
        c.wait()
    even = sec % 2 == 0
    up, down, fill_low, fill_high = [], [], [], []
    for p, part in enumerate(PARTS):
        rows, held = pl.ds(*part), near[p]
        up.append(remote(held.at[1], held.at[0], psi_send.at[p, 0], psi_recv.at[p, 0], at_sec(1)))
        down.append(remote(held.at[1], held.at[2], psi_send.at[p, 1], psi_recv.at[p, 1], at_sec(-1)))
        fill_low.append(pltpu.make_async_copy(psi.at[0, rows], held.at[0], psi_recv.at[p, 0]))
        fill_high.append(pltpu.make_async_copy(psi.at[0, rows], held.at[2], psi_recv.at[p, 1]))
    for p in range(len(PARTS)):
        pl.when(even & has_down)(down[p].start)
        pl.when(jnp.logical_not(even) & has_up)(up[p].start)
    for p in range(len(PARTS)):
        pl.when(even)(up[p].start)
        pl.when(jnp.logical_not(even))(down[p].start)
        pl.when(sec == 0)(fill_low[p].start)
        pl.when(sec == NSEC - 1)(fill_high[p].start)
    for peer in beside:
        signal(know_a, peer)
    for c in loads:
        c.start()
    pl.semaphore_wait(know_a, 4)
    for d in (2, -2):
        signal(know_b, at_z(d))
    for c in loads:
        c.wait()

    live = count[0, 0]
    for p, (first, rows) in enumerate(PARTS):
        pl.when(has_down)(up[p].wait_recv)
        pl.when(has_up)(down[p].wait_recv)
        pl.when(sec == 0)(fill_low[p].wait)
        pl.when(sec == NSEC - 1)(fill_high[p].wait)
        for t in range(SLOTS):
            block = near[p][jnp.clip(src[t] - sec + 1, 0, 2)]
            inner = jnp.dot(block, rbuf[t], preferred_element_type=jnp.float32)
            inner = jnp.where(t < live, inner, 0.0).astype(jnp.bfloat16)
            icat[pl.ds(SLOTS * first + t * rows, rows)] = inner
        span = pl.ds(SLOTS * first, SLOTS * rows)
        term = jnp.dot(lbuf[:, span], icat[span], preferred_element_type=jnp.float32)
        if p == 0:
            acc[...] = term
    total = acc[...] + term
    pbuf[...] = total.astype(jnp.bfloat16).reshape(NY, NB, OWN, ROWS, M)

    y_copies = []
    for i, b in enumerate(blocks):
        row = []
        for d in Y_FIRST:
            c = remote(
                pbuf.at[(y + d) % NY, b], yrecv.at[d - 1, b],
                ys_sem.at[d - 1, i], yr_sem.at[d - 1, i], at_y(d),
            )
            c.start()
            row.append(c)
        y_copies.append(row)
    pl.semaphore_wait(know_b, 2)
    for d in (4, -4):
        signal(know_c, at_z(d))

    def piece(i, k):
        b = blocks[i]
        owner = (FIRST + b * OWN + k) % NZ
        copy = remote(
            zbuf.at[b, k], zrecv.at[z], zs_sem.at[i, k], zr_sem.at[z], (owner * NY + y, sec)
        )
        return owner != z, copy

    for i, b in enumerate(blocks):
        for c in y_copies[i]:
            c.wait_recv()
        total = pbuf[y, b].astype(jnp.float32)
        for d in range(1, NY):
            total = total + yrecv[d - 1, b].astype(jnp.float32)
        zbuf[b] = total.astype(jnp.bfloat16)
        if i == 0:
            pl.semaphore_wait(know_c, 2)
        for k in range(OWN):
            other, c = piece(i, k)
            pl.when(other)(c.start)

    def spread(s):
        part = quarter.at[mb, mk]
        return remote(part, part, gs_sem.at[s], gr_sem.at[mb, mk], (s * NY + y, sec))

    @pl.when(is_owner)
    def _():
        total = zbuf[mb, mk].astype(jnp.float32)
        for d in NEAR_FIRST:
            s = (z + d) % NZ
            remote(zbuf.at[0, 0], zrecv.at[s], zs_sem.at[0, 0], zr_sem.at[s], at_z(1)).wait_recv()
            total = total + zrecv[s].astype(jnp.float32)
        quarter[mb, mk] = total.astype(jnp.bfloat16)
        for s in SPREAD:
            pl.when(s != z)(spread(s).start)

    h_copies = []
    for i, b in reversed(list(enumerate(blocks))):
        for k in range(OWN):
            part = quarter.at[b, k]
            arrival = remote(part, part, gs_sem.at[0], gr_sem.at[b, k], at_z(1))
            pl.when(b * OWN + k != mine)(arrival.wait_recv)
        for d in Y_FIRST:
            c = remote(
                quarter.at[b], out.at[y, b], hs_sem.at[d - 1, b], hr_sem.at[d - 1, b], at_y(d)
            )
            c.start()
            h_copies.append(c)
        c = pltpu.make_async_copy(quarter.at[b], out.at[y, b], out_sem.at[b])
        c.start()
        h_copies.append(c)

    for p in range(len(PARTS)):
        pl.when(has_up)(up[p].wait_send)
        pl.when(has_down)(down[p].wait_send)
    for row in y_copies:
        for c in row:
            c.wait_send()
    for i in range(NB):
        for k in range(OWN):
            other, c = piece(i, k)
            pl.when(other)(c.wait_send)

    @pl.when(is_owner)
    def _():
        for s in SPREAD:
            pl.when(s != z)(spread(s).wait_send)

    for c in h_copies:
        c.wait()


def local(psi, left_ops, right_ops, term_src, term_count):
    hbm = pl.BlockSpec(memory_space=pl.ANY)
    dma, plain = pltpu.SemaphoreType.DMA, pltpu.SemaphoreType.REGULAR
    bf16 = jnp.bfloat16
    out = pl.pallas_call(
        kernel,
        out_shape=jax.ShapeDtypeStruct((NY, NB, OWN, ROWS, M), bf16),
        in_specs=[hbm, hbm, hbm, hbm, hbm],
        out_specs=hbm,
        scratch_shapes=[
            pltpu.SMEM((SLOTS,), jnp.int32),
            pltpu.SMEM((1, 1), jnp.int32),
            *(pltpu.VMEM((3, rows, M), bf16) for first, rows in PARTS),
            pltpu.VMEM((M, SLOTS * M), bf16),
            pltpu.VMEM((SLOTS, M, M), bf16),
            pltpu.VMEM((SLOTS * M, M), bf16),
            pltpu.VMEM((M, M), jnp.float32),
            pltpu.VMEM((NY, NB, OWN, ROWS, M), bf16),
            pltpu.VMEM((NY - 1, NB, OWN, ROWS, M), bf16),
            pltpu.VMEM((NB, OWN, ROWS, M), bf16),
            pltpu.VMEM((NZ, ROWS, M), bf16),
            pltpu.VMEM((NB, OWN, ROWS, M), bf16),
            dma((2,)), dma((2, SLOTS)), dma((SLOTS,)), dma((2, 2)), dma((2, 2)),
            dma((NY - 1, NB)), dma((NY - 1, NB)),
            dma((NB, OWN)), dma((NZ,)),
            dma((NZ,)), dma((NB, OWN)),
            dma((NY - 1, NB)), dma((NY - 1, NB)), dma((NB,)),
            plain, plain, plain, dma((2,)),
        ],
        compiler_params=pltpu.CompilerParams(
            collective_id=0, has_side_effects=True, vmem_limit_bytes=60 * 1024 * 1024
        ),
        cost_estimate=pl.CostEstimate(
            flops=4 * SLOTS * M**3, bytes_accessed=4 * SLOTS * M * M, transcendentals=0
        ),
        name="sigma_sum",
    )(psi, left_ops, right_ops, term_src, term_count)
    return out.reshape(1, M, M)


def solution(mesh):
    in_specs = (
        P("sec", None, None),
        P(("op", "sec"), None, None),
        P(("op", "sec"), None, None),
        P(("op", "sec")),
        P("op", "sec"),
    )
    out_specs = P("sec", None, None)
    return jax.shard_map(local, mesh=mesh, in_specs=in_specs, out_specs=out_specs, check_vma=False)
```

time: 46.7 us -> 45 us (0.964)
  the two profiles are of different devices: /device:TPU:6 before, /device:TPU:68 now
where the time goes in v3:
time: 45 us; the launch traced here: 44.8 us
  Pallas kernels  42.4 us (94%)
  local copies, waits for them, and re-layouts  1.71 us (4%)
  between operations  0.66 us (1%)
    pallas_call x1, Pallas kernels, local(): pl.pallas_call(kernel, out_shape=jax.ShapeDtypeStruct((NY, NB, OWN, ROWS,...  42.4 us
    unnamed x1, local copies, waits for them, and re-layouts  1.71 us

profile of v3, /device:TPU:68, one launch (start us, length us, event | category | flops | bytes accessed | tf_op | source)
XLA Modules:
  0.0 44.8 jit_solution(17711476905251121157)
XLA Ops:
  0.7 42.4 %sigma_sum.1 = bf16[4,4,3,8,384]{4,3,2,1,0:T(8,128)(2,1)} custom-call(bf16[1,384,384]{2,1,0:T(8,128)(2,1)} %psi.1, bf16[7,384,384]{2,1,0:T(8,128)(2,1)} %left.1, bf16[7,384,384]{2,1,0:T(8,128)(2,1)} %right.1, s32[7]{0:T(128)} %src_in.1, s32[1,1]{1,0:T(1,128)S(6)} %copy.7.count_in), custom_call_target="tpu_custom_call" | custom-call | flops 1585446912 | bytes 4128768 | tf_op jit(solution)/shard_map/sigma_sum/pallas_call | solution.py:233
  43.1 1.7 %copy.8 = bf16[1,384,384]{2,1,0:T(8,128)(2,1)} copy(bf16[1,384,384]{2,1,0:T(8,128)(2,1)} %bitcast.1) | data formatting | bytes 589824

commit v4 on v3

--- a/solution.py
+++ b/solution.py
@@ -127,6 +127,10 @@
         pl.when(has_up)(down[p].wait_recv)
         pl.when(sec == 0)(fill_low[p].wait)
         pl.when(sec == NSEC - 1)(fill_high[p].wait)
+        if p == 1:
+            pl.semaphore_wait(know_b, 2)
+            for d in (4, -4):
+                signal(know_c, at_z(d))
         for t in range(SLOTS):
             block = near[p][jnp.clip(src[t] - sec + 1, 0, 2)]
             inner = jnp.dot(block, rbuf[t], preferred_element_type=jnp.float32)
@@ -150,9 +154,6 @@
             c.start()
             row.append(c)
         y_copies.append(row)
-    pl.semaphore_wait(know_b, 2)
-    for d in (4, -4):
-        signal(know_c, at_z(d))
 
     def piece(i, k):
         b = blocks[i]

time: 45 us -> 44.4 us (0.987)
  Pallas kernels: 42.4 us -> 41.8 us
    pallas_call x1, Pallas kernels: 42.4 us -> 41.8 us  [local(): pl.pallas_call(kernel, out_shape=jax.ShapeDtypeStruct((NY, NB, OWN, ROWS,...]
where the time goes in v4:
time: 44.4 us; the launch traced here: 44.2 us
  Pallas kernels  41.8 us (94%)
  local copies, waits for them, and re-layouts  1.71 us (4%)
  between operations  0.66 us (1%)
    pallas_call x1, Pallas kernels, local(): pl.pallas_call(kernel, out_shape=jax.ShapeDtypeStruct((NY, NB, OWN, ROWS,...  41.8 us
    unnamed x1, local copies, waits for them, and re-layouts  1.71 us

profile of v4, /device:TPU:68, one launch (start us, length us, event | category | flops | bytes accessed | tf_op | source)
XLA Modules:
  0.0 44.2 jit_solution(3744541321133142464)
XLA Ops:
  0.7 41.8 %sigma_sum.1 = bf16[4,4,3,8,384]{4,3,2,1,0:T(8,128)(2,1)} custom-call(bf16[1,384,384]{2,1,0:T(8,128)(2,1)} %psi.1, bf16[7,384,384]{2,1,0:T(8,128)(2,1)} %left.1, bf16[7,384,384]{2,1,0:T(8,128)(2,1)} %right.1, s32[7]{0:T(128)} %src_in.1, s32[1,1]{1,0:T(1,128)S(6)} %copy.7.count_in), custom_call_target="tpu_custom_call" | custom-call | flops 1585446912 | bytes 4128768 | tf_op jit(solution)/shard_map/sigma_sum/pallas_call | solution.py:234
  42.5 1.7 %copy.8 = bf16[1,384,384]{2,1,0:T(8,128)(2,1)} copy(bf16[1,384,384]{2,1,0:T(8,128)(2,1)} %bitcast.1) | data formatting | bytes 589824

commit v5 on v4

--- a/solution.py
+++ b/solution.py
@@ -23,7 +23,7 @@
     near_a, near_b, lbuf, rbuf, icat, acc, pbuf, yrecv, zbuf, zrecv, quarter,
     psi_sem, l_sem, r_sem, psi_send, psi_recv,
     ys_sem, yr_sem, zs_sem, zr_sem, gs_sem, gr_sem, hs_sem, hr_sem, out_sem,
-    know_a, know_b, know_c, scalar_sem,
+    know_a, know_b, know_c, scalar_sem, fs_sem, fr_sem,
 ):
     op, sec = lax.axis_index("op"), lax.axis_index("sec")
     z, y = op // NY, op % NY
@@ -197,7 +197,14 @@
             part = quarter.at[b, k]
             arrival = remote(part, part, gs_sem.at[0], gr_sem.at[b, k], at_z(1))
             pl.when(b * OWN + k != mine)(arrival.wait_recv)
-        for d in Y_FIRST:
+            if i == 0:
+                for d in Y_FIRST:
+                    c = remote(
+                        part, out.at[y, b, k], fs_sem.at[d - 1, k], fr_sem.at[d - 1, k], at_y(d)
+                    )
+                    c.start()
+                    h_copies.append(c)
+        for d in Y_FIRST if i else ():
             c = remote(
                 quarter.at[b], out.at[y, b], hs_sem.at[d - 1, b], hr_sem.at[d - 1, b], at_y(d)
             )
@@ -254,7 +261,7 @@
             dma((NB, OWN)), dma((NZ,)),
             dma((NZ,)), dma((NB, OWN)),
             dma((NY - 1, NB)), dma((NY - 1, NB)), dma((NB,)),
-            plain, plain, plain, dma((2,)),
+            plain, plain, plain, dma((2,)), dma((NY - 1, OWN)), dma((NY - 1, OWN)),
         ],
         compiler_params=pltpu.CompilerParams(
             collective_id=0, has_side_effects=True, vmem_limit_bytes=60 * 1024 * 1024

time: 44.4 us -> 44.7 us (level)
  no operation moved by 1% of the time
where the time goes in v5:
time: 44.7 us; the launch traced here: 44.5 us
  Pallas kernels  42.1 us (94%)
  local copies, waits for them, and re-layouts  1.71 us (4%)
  between operations  0.66 us (1%)
    pallas_call x1, Pallas kernels, local(): pl.pallas_call(kernel, out_shape=jax.ShapeDtypeStruct((NY, NB, OWN, ROWS,...  42.1 us
    unnamed x1, local copies, waits for them, and re-layouts  1.71 us

profile of v5, /device:TPU:68, one launch (start us, length us, event | category | flops | bytes accessed | tf_op | source)
XLA Modules:
  0.0 44.5 jit_solution(118937387242407960)
XLA Ops:
  0.7 42.1 %sigma_sum.1 = bf16[4,4,3,8,384]{4,3,2,1,0:T(8,128)(2,1)} custom-call(bf16[1,384,384]{2,1,0:T(8,128)(2,1)} %psi.1, bf16[7,384,384]{2,1,0:T(8,128)(2,1)} %left.1, bf16[7,384,384]{2,1,0:T(8,128)(2,1)} %right.1, s32[7]{0:T(128)} %src_in.1, s32[1,1]{1,0:T(1,128)S(6)} %copy.7.count_in), custom_call_target="tpu_custom_call" | custom-call | flops 1585446912 | bytes 4128768 | tf_op jit(solution)/shard_map/sigma_sum/pallas_call | solution.py:241
  42.8 1.7 %copy.8 = bf16[1,384,384]{2,1,0:T(8,128)(2,1)} copy(bf16[1,384,384]{2,1,0:T(8,128)(2,1)} %bitcast.1) | data formatting | bytes 589824
